TPU v7x, 32 devices: a whole 2x2x4 slice. The times are simulated.
32 devices in a mesh: wide: 4 (over x, core), rep: 8 (over z, y).
Axes of the slice: x: 2, y: 2, z: 4, core: 2. Of those that a mesh axis runs over, the one named last changes fastest.
Arguments:
- stretch_qkv: bfloat16 [8, 1536, 3, 5120], P('rep', 'wide'), may hold values from -60 to 60
- norm_gains: float32 [2, 5120], replicated, may hold values from 0.25 to 1.75
- cache: bfloat16 [128, 2, 192, 5120], P('rep', None, 'wide'), may hold values from -6 to 6
- cached_stretches: int32 [8], replicated, may hold values from 1 to 2, as said below
- block_slot: int32 [8, 16], replicated, may hold values from 0 to 127, as said below
- video_of_group: int32 [8], replicated, may hold values from 0 to 7, each once
Outputs:
- attended: bfloat16 [8, 1536, 5120], P('rep', 'wide')
Inputs may be any that keep to these rules, and one draw needn't show every extreme that they name: `cached_stretches`: each value is 1 to 2; some video has exactly 2. Block b of video u holds that video's cached tokens b * 192 to (b + 1) * 192 - 1, oldest first; it is cache row block_slot[u, b], owned by group block_slot[u, b] // 16. Every group owns exactly 2 blocks of every video; no two blocks share a row.
All inputs are finite; a program needn't handle non-finite values.
Results may differ from a plain program's by a relative error of at most 0.011.
Values may be sent and summed in bfloat16 or wider, within the bound.
No kernel may reach another device: no remote copies, remote signals or barrier semaphores. Data moves between devices by JAX's collectives and lax.ppermute only.
A program may use at most 192 MiB of HBM per device.

v0:
```python
import functools
import math

import jax
import jax.numpy as jnp
from jax import lax
from jax.experimental import pallas as pl
from jax.experimental.pallas import tpu as pltpu
from jax.sharding import Mesh, PartitionSpec as P

HD = 128
EPS = 1e-06
STAT_ROWS = 16
VMEM_LIMIT = 56 * 1024 * 1024
CHUNKS = (8, 6, 4, 2)


def own_blocks(own_group, slots_ref, videos_ref, slots_dev, visit):
    def each_group(group, carry):
        video = videos_ref[group]

        def each_block(block, rank):
            slot = slots_ref[video, block]
            mine = slot // slots_dev == own_group
            pl.when(mine)(functools.partial(visit, group, rank, slot - own_group * slots_dev))
            return rank + mine.astype(jnp.int32)

        lax.fori_loop(0, slots_ref.shape[1], each_block, jnp.int32(0), unroll=True)
        return carry

    lax.fori_loop(0, videos_ref.shape[0], each_group, jnp.int32(0))


def pack_kernel(cap, head0, width, half, place_ref, slots_ref, videos_ref, cache_ref, out_ref, sems):
    groups = videos_ref.shape[0]

    def copy_of(slot, group, rank, core):
        return pltpu.make_async_copy(
            cache_ref.at[slot, :, :, pl.ds(core * half + head0 * HD, width)],
            out_ref.at[core * groups + group, :, rank],
            sems.at[(group * cap + rank) * 2 + core],
        )

    def visit(group, rank, slot):
        @pl.when(rank < cap)
        def _():
            for core in range(2):
                copy_of(slot, group, rank, core).start()

    own_blocks(place_ref[0], slots_ref, videos_ref, cache_ref.shape[0], visit)
    for group in range(groups):
        for rank in range(cap):
            for core in range(2):
                copy_of(0, group, rank, core).wait()


def pack(cache, place, slots, videos, cap, head0, heads):
    groups = videos.shape[0]
    width = heads * HD
    half = cache.shape[-1] // 2
    shape = (2 * groups, 2, cap, cache.shape[2], width)
    return pl.pallas_call(
        functools.partial(pack_kernel, cap, head0, width, half),
        out_shape=jax.ShapeDtypeStruct(shape, cache.dtype),
        grid_spec=pltpu.PrefetchScalarGridSpec(
            num_scalar_prefetch=3,
            grid=(1,),
            in_specs=[pl.BlockSpec(memory_space=pl.ANY)],
            out_specs=pl.BlockSpec(shape, lambda i, *_: (0, 0, 0, 0, 0)),
            scratch_shapes=[pltpu.SemaphoreType.DMA((2 * groups * cap,))],
        ),
        compiler_params=pltpu.CompilerParams(vmem_limit_bytes=VMEM_LIMIT),
        cost_estimate=pl.CostEstimate(flops=0, bytes_accessed=4 * math.prod(shape), transcendentals=0),
        name="pack",
    )(place, slots, videos, cache)


def norm_kernel(half, place_ref, qkv_ref, gains_ref, *out_refs):
    core = place_ref[1]

    def normed(which):
        widened = qkv_ref[which].astype(jnp.float32)
        mean_square = jnp.mean(widened * widened, axis=-1, keepdims=True)
        return (widened * lax.rsqrt(mean_square + EPS) * gains_ref[which : which + 1, :]).astype(jnp.bfloat16)

    rows = (normed(0), normed(1), qkv_ref[2])

    def put(own):
        for which in range(3):
            out_refs[2 * which][...] = rows[which][:, own * half : (own + 1) * half]
            out_refs[2 * which + 1][...] = rows[which][:, (1 - own) * half : (2 - own) * half]

    @pl.when(core == 0)
    def _():
        put(0)

    @pl.when(core != 0)
    def _():
        put(1)


def norm(qkv, gains, place):
    _, tokens, width = qkv.shape
    half = width // 2
    block = math.gcd(tokens, 64)
    out = jax.ShapeDtypeStruct((tokens, half), jnp.bfloat16)
    return pl.pallas_call(
        functools.partial(norm_kernel, half),
        out_shape=[out] * 6,
        grid_spec=pltpu.PrefetchScalarGridSpec(
            num_scalar_prefetch=1,
            grid=(tokens // block,),
            in_specs=[
                pl.BlockSpec((3, block, width), lambda i, p: (0, i, 0)),
                pl.BlockSpec((2, width), lambda i, p: (0, 0)),
            ],
            out_specs=[pl.BlockSpec((block, half), lambda i, p: (i, 0))] * 6,
        ),
        compiler_params=pltpu.CompilerParams(vmem_limit_bytes=VMEM_LIMIT),
        cost_estimate=pl.CostEstimate(flops=8 * tokens * width, bytes_accessed=12 * tokens * width, transcendentals=tokens),
        name="norm",
    )(place, qkv, gains)


def attend_kernel(heads, pieces, bias_ref, kc_ref, vc_ref, *refs):
    q_refs = refs[:pieces]
    kn_refs = refs[pieces : pieces + 2]
    vn_refs = refs[pieces + 2 : pieces + 4]
    out_refs = refs[pieces + 4 : 2 * pieces + 4]
    k_ref, v_ref = refs[2 * pieces + 4 :]
    head = pl.program_id(0)
    cached = bias_ref.shape[1]
    tokens = kn_refs[0].shape[0]

    @pl.when(head == 0)
    def _():
        v_ref[:, HD:] = jnp.ones_like(v_ref[:, HD:])

    def put(at, rows, keys, values):
        k_ref[at : at + rows, :HD] = keys
        k_ref[at : at + rows, HD:] = keys
        v_ref[at : at + rows, :HD] = values

    put(0, cached, kc_ref[...].reshape(cached, HD), vc_ref[...].reshape(cached, HD))
    at = cached
    for i in range(2):
        put(at, tokens, kn_refs[i][...], vn_refs[i][...])
        at += tokens
    factor = math.log2(math.e) * HD ** (-0.5)
    segment = tokens // 3
    row = lax.broadcasted_iota(jnp.int32, (STAT_ROWS, HD), 0)

    def scores_of(q_ref):
        scaled = q_ref[...].astype(jnp.float32) * factor
        high = scaled.astype(jnp.bfloat16)
        low = (scaled - high.astype(jnp.float32)).astype(jnp.bfloat16)
        query = jnp.concatenate([high, low], axis=1)
        return lax.dot_general(query, k_ref[...], (((1,), (1,)), ((), ())), preferred_element_type=jnp.float32)

    def finish(scores, out_ref):
        scores = jnp.concatenate([scores[:, :cached] + bias_ref[...], scores[:, cached:]], axis=1)
        row_max = jnp.max(scores, axis=-1, keepdims=True)
        weights = jnp.exp2(scores - row_max).astype(jnp.bfloat16)
        mixed = jnp.dot(weights, v_ref[...], preferred_element_type=jnp.float32)
        row_total = mixed[:, HD:]
        columns = pl.ds(pl.multiple_of(head * HD, HD), HD)
        out_ref[:tokens, columns] = (mixed[:, :HD] / row_total).astype(jnp.bfloat16)
        level = row_max + jnp.log2(row_total)
        tile = jnp.zeros((STAT_ROWS, HD), jnp.float32)
        for part in range(3):
            flat = jnp.transpose(level[part * segment : (part + 1) * segment])[:STAT_ROWS]
            if segment < HD:
                flat = jnp.concatenate([flat, jnp.zeros((STAT_ROWS, HD - segment), jnp.float32)], axis=1)
            high = flat.astype(jnp.bfloat16).astype(jnp.float32)
            middle = (flat - high).astype(jnp.bfloat16).astype(jnp.float32)
            tile = jnp.where(row == part, high, tile)
            tile = jnp.where(row == 3 + part, middle, tile)
            tile = jnp.where(row == 6 + part, flat - high - middle, tile)
        out_ref[tokens:, columns] = tile.astype(jnp.bfloat16)

    scores = scores_of(q_refs[0])
    for i in range(pieces):
        following = scores_of(q_refs[i + 1]) if i + 1 < pieces else None
        finish(scores, out_refs[i])
        scores = following


def attend(bias, arrived, queries, new_keys, new_values, head0, heads):
    pieces = len(queries)
    tokens = queries[0][0].shape[0]
    cached = bias.shape[1]
    keys = cached + 2 * tokens
    sources, _, rows, _ = arrived.shape

    def column(first):
        return pl.BlockSpec((tokens, HD), lambda h: (0, head0 - first + h))

    in_specs = [
        pl.BlockSpec((1, cached), lambda h: (0, 0)),
        pl.BlockSpec((sources, None, rows, HD), lambda h: (0, 0, 0, h)),
        pl.BlockSpec((sources, None, rows, HD), lambda h: (0, 1, 0, h)),
    ]
    operands = [bias, arrived, arrived]
    for array, first in queries:
        in_specs.append(column(first))
        operands.append(array)
    for array in (*new_keys, *new_values):
        in_specs.append(column(0))
        operands.append(array)
    out = jax.ShapeDtypeStruct((tokens + STAT_ROWS, heads * HD), jnp.bfloat16)
    work = pieces * tokens * keys * heads
    return pl.pallas_call(
        functools.partial(attend_kernel, heads, pieces),
        out_shape=[out] * pieces,
        grid=(heads,),
        in_specs=in_specs,
        out_specs=[pl.BlockSpec((tokens + STAT_ROWS, heads * HD), lambda h: (0, 0))] * pieces,
        scratch_shapes=[pltpu.VMEM((keys, 2 * HD), jnp.bfloat16)] * 2,
        compiler_params=pltpu.CompilerParams(vmem_limit_bytes=VMEM_LIMIT),
        cost_estimate=pl.CostEstimate(flops=8 * HD * work, bytes_accessed=4 * keys * heads * HD + 4 * pieces * tokens * heads * HD, transcendentals=work),
        name="attend",
    )(*operands)


def merge_kernel(heads, x_count, head0, place_ref, *refs):
    parts = refs[: 2 * x_count]
    whole_ref, joined_ref, sems = refs[-3:]
    half_width = whole_ref.shape[1] // 2
    tokens = whole_ref.shape[0]
    segment = tokens // 3
    row = lax.broadcasted_iota(jnp.int32, (STAT_ROWS, HD), 0)
    copies = []
    for side in range(2):
        for head in range(heads):
            columns = slice(head * HD, (head + 1) * HD)
            for part in range(3):
                own = (row == part) | (row == 3 + part) | (row == 6 + part)
                rows = slice(part * segment, (part + 1) * segment)
                levels = [
                    lax.dot_general(
                        parts[dx * 2 + side][tokens:, columns][:, :segment],
                        own.astype(jnp.bfloat16),
                        (((0,), (0,)), ((), ())),
                        preferred_element_type=jnp.float32,
                    )
                    for dx in range(x_count)
                ]
                top = functools.reduce(jnp.maximum, levels)
                shares = [jnp.exp2(level - top) for level in levels]
                total = sum(shares)
                joined = sum(
                    shares[dx] * parts[dx * 2 + side][rows, columns].astype(jnp.float32) for dx in range(x_count)
                )
                joined_ref[side, rows, columns] = (joined / total).astype(joined_ref.dtype)
        core = place_ref[1] if side == 0 else 1 - place_ref[1]
        start = pl.multiple_of(core * half_width + head0 * HD, HD)
        copy = pltpu.make_async_copy(joined_ref.at[side], whole_ref.at[:, pl.ds(start, heads * HD)], sems.at[side])
        copy.start()
        copies.append(copy)
    for copy in copies:
        copy.wait()


def merge(parts, place, whole, width, head0, heads):
    tokens = parts[0].shape[0] - STAT_ROWS
    in_specs = [pl.BlockSpec(part.shape, lambda i, *_: (0, 0)) for part in parts]
    operands = list(parts)
    aliases = {}
    if whole is not None:
        in_specs.append(pl.BlockSpec(memory_space=pl.ANY))
        operands.append(whole)
        aliases = {len(operands): 0}
    return pl.pallas_call(
        functools.partial(merge_kernel, heads, len(parts) // 2, head0),
        out_shape=jax.ShapeDtypeStruct((tokens, width), jnp.bfloat16),
        grid_spec=pltpu.PrefetchScalarGridSpec(
            num_scalar_prefetch=1,
            grid=(1,),
            in_specs=in_specs,
            out_specs=pl.BlockSpec(memory_space=pl.ANY),
            scratch_shapes=[pltpu.VMEM((2, tokens, heads * HD), jnp.bfloat16), pltpu.SemaphoreType.DMA((2,))],
        ),
        input_output_aliases=aliases,
        compiler_params=pltpu.CompilerParams(vmem_limit_bytes=VMEM_LIMIT),
        cost_estimate=pl.CostEstimate(flops=8 * tokens * heads * HD * len(parts), bytes_accessed=4 * tokens * heads * HD * len(parts), transcendentals=0),
        name="merge",
    )(place, *operands)


def plan_chunks(heads):
    sizes = CHUNKS if sum(CHUNKS) == heads else (heads,)
    starts = [sum(sizes[:i]) for i in range(len(sizes))]
    return list(zip(starts, sizes))


def body(stretch_qkv, norm_gains, cache, cached_stretches, block_slot, video_of_group):
    x_count = lax.axis_size("x")
    groups = lax.axis_size("rep")
    own_group = lax.axis_index("rep")
    core = lax.axis_index("core")
    place = jnp.stack([own_group, core]).astype(jnp.int32)
    qkv = jnp.transpose(stretch_qkv[0], (1, 0, 2))
    _, tokens, width = qkv.shape
    half = width // 2
    slots_dev, _, block_wide, _ = cache.shape
    cap = slots_dev // groups
    blocks = block_slot.shape[1]
    stretch = tokens * 2 * x_count
    block_len = block_wide * 2 * x_count
    chunks = plan_chunks(half // HD)
    offsets = [(dx, dc) for dx in range(x_count) for dc in range(2)]

    def move(value, dx, dc, back=False):
        if dx == 0 and dc == 0:
            return value
        pairs = []
        for x in range(x_count):
            for c in range(2):
                here, there = x * 2 + c, ((x + dx) % x_count) * 2 + (c + dc) % 2
                pairs.append((there, here) if back else (here, there))
        return lax.ppermute(value, ("x", "core"), pairs)

    def tie(value, *others):
        return lax.optimization_barrier((value, *others))[0]

    def spread_out(index, *earlier):
        head0, heads = chunks[index]
        sent = pack(cache, place, block_slot, video_of_group, cap, head0, heads)
        if earlier:
            sent = tie(sent, *earlier)
        got = lax.all_to_all(sent, ("core", "rep"), split_axis=0, concat_axis=0, tiled=True)
        rows = cap * block_wide
        got = got.reshape(2 * groups, 2, rows, heads * HD)
        if rows % 16:
            got = jnp.transpose(got, (1, 0, 2, 3)).reshape(1, 2, 2 * groups * rows, heads * HD)
        return got

    got = spread_out(0)

    own_video = video_of_group[own_group]
    own_slots = block_slot[own_video]
    owners = own_slots // slots_dev
    order = jnp.arange(blocks, dtype=jnp.int32)
    rank = jnp.sum(((owners[:, None] == owners[None, :]) & (order[:, None] > order[None, :])).astype(jnp.int32), axis=1)
    shown = order * block_len < cached_stretches[own_video] * stretch
    unit = owners * cap + rank
    shown_unit = jnp.any((unit[:, None] == jnp.arange(groups * cap)[None, :]) & shown[:, None], axis=0)
    bias = jnp.where(shown_unit, 0.0, -jnp.inf).astype(jnp.float32)
    bias = jnp.broadcast_to(bias[None, :, None], (2, groups * cap, block_wide)).reshape(1, -1)

    q_own, q_far, k_own, k_far, v_own, v_far = norm(qkv, norm_gains, place)
    new_keys = [k_own, move(k_far, 0, 1)]
    new_values = [v_own, move(v_far, 0, 1)]
    early = chunks[0][1]
    early_queries = [move((q_far if dc else q_own)[:, : early * HD], dx, dc) for dx, dc in offsets]
    late_queries = []
    if len(chunks) > 1:
        late_queries = [move((q_far if dc else q_own)[:, early * HD :], dx, dc) for dx, dc in offsets]

    wholes = []
    held, done = [*early_queries, new_keys[1], new_values[1]], []
    for index, (head0, heads) in enumerate(chunks):
        last = index + 1 == len(chunks)
        following = None if last else spread_out(index + 1, got, *held, *done)
        queries = [(array, early if index else 0) for array in (late_queries if index else early_queries)]
        near = pieces = len(offsets)
        if last and len(chunks) > 2:
            near = 2
            got = tie(got, wholes[-2])
        far_outs = attend(bias, got, queries[near:], new_keys, new_values, head0, heads) if near < pieces else []
        own_outs = attend(bias, got, queries[:near], new_keys, new_values, head0, heads)
        outs = [*own_outs, *far_outs]
        parts = [move(out, dx, dc, back=True) for out, (dx, dc) in zip(outs, offsets)]
        done = wholes[-1:]
        wholes.append(merge(parts, place, wholes[-1] if wholes else None, width, head0, heads))
        held = parts + (late_queries if index == 0 else [])
        got = following
    return wholes[-1][None]


def solution(mesh):
    wide, rep = mesh.devices.shape
    fine = Mesh(mesh.devices.reshape(wide // 2, 2, rep), ("x", "core", "rep"))
    wide_axes = ("x", "core")
    in_specs = (P("rep", wide_axes, None, None), P(), P("rep", None, wide_axes, None), P(), P(), P())
    out_specs = P("rep", wide_axes, None)
    return jax.shard_map(body, mesh=fine, in_specs=in_specs, out_specs=out_specs, check_vma=False)
```

profile of v0, /device:TPU:0, one launch (start us, length us, event | category | flops | bytes accessed | tf_op | source)
XLA Modules:
  0.0 404.4 jit_solution(1617343247815718601)
XLA Ops:
  0.6 7.0 %pack.7 = bf16[16,2,2,48,1024]{4,3,2,1,0:T(8,128)(2,1)} custom-call(s32[2]{0:T(128)} %pad_add_fusion.place_ref, s32[8,16]{1,0:T(8,128)} %slots_ref.7, s32[8]{0:T(128)} %videos_ref.7, bf16[16,2,48,5120]{3,2,1,0:T(8,128)(2,1)} %cache_ref.7), custom_call_target="tpu_custom_call" | custom-call | bytes 12582912 | tf_op jit(solution)/shard_map/pack/pallas_call | solution.py:62
  7.6 7.5 %all-to-all-start = ((bf16[16,2,2,48,1024]{4,3,2,1,0:T(8,128)(2,1)}), bf16[16,2,2,48,1024]{4,3,2,1,0:T(8,128)(2,1)}, u32[]{:S(2)}, u32[]{:S(2)}) async-start(bf16[16,2,2,48,1024]{4,3,2,1,0:T(8,128)(2,1)} %pack.7), calls=%async_computation | async-start | bytes 12582912 | tf_op jit(solution)/shard_map/all_to_all | solution.py:331
  15.1 12.8 %norm.1 = (bf16[384,2560]{1,0:T(8,128)(2,1)}, bf16[384,2560]{1,0:T(8,128)(2,1)}, bf16[384,2560]{1,0:T(8,128)(2,1)}, bf16[384,2560]{1,0:T(8,128)(2,1)}, bf16[384,...) custom-call(s32[2]{0:T(128)} %pad_add_fusion.place_ref, bf16[3,384,5120]{2,1,0:T(8,128)(2,1)} %bitcast.24, f32[2,5120]{1,0:T(2,128)} %gains_ref.1), custom_call_target="tpu_custom_call" | custom-call | flops 15728640 | bytes 23592960 | tf_op jit(solution)/shard_map/norm/pallas_call | solution.py:107
  28.4 1.2 slice.16.refs_0_
  29.6 1.6 collective-permute-start.1
  31.2 1.2 slice.17
  33.1 6.4 %pack.6 = bf16[16,2,2,48,768]{4,3,2,1,0:T(8,128)(2,1)} custom-call(s32[2]{0:T(128)} %pad_add_fusion.place_ref, s32[8,16]{1,0:T(8,128)} %slots_ref.7, s32[8]{0:T(128)} %videos_ref.7, bf16[16,2,48,5120]{3,2,1,0:T(8,128)(2,1)} %cache_ref.7), custom_call_target="tpu_custom_call" | custom-call | bytes 9437184 | tf_op jit(solution)/shard_map/pack/pallas_call | solution.py:62
  39.5 10.5 %collective-permute-done.1.refs_2_ = bf16[384,1024]{1,0:T(8,128)(2,1)S(1)} collective-permute-done((bf16[384,1024]{1,0:T(8,128)(2,1)S(1)}, bf16[384,1024]{1,0:T(8,128)(2,1)S(1)}, u32[]{:S(2)}, u32[]{:S(2)}) %collective-permute-start.1) | collective-permute-done | bytes 786464 | tf_op jit(solution)/shard_map/ppermute | solution.py:321
  50.1 15.7 %collective-permute-done.2.refs_3_ = bf16[384,1024]{1,0:T(8,128)(2,1)S(1)} collective-permute-done((bf16[384,1024]{1,0:T(8,128)(2,1)S(1)}, bf16[384,1024]{1,0:T(8,128)(2,1)S(1)}, u32[]{:S(2)}, u32[]{:S(2)}) %collective-permute-start.2) | collective-permute-done | bytes 786464 | tf_op jit(solution)/shard_map/ppermute | solution.py:321
  65.8 0.9 copy-done.16
  66.7 80.4 %all-to-all-done = bf16[16,2,2,48,1024]{4,3,2,1,0:T(8,128)(2,1)} async-done(((bf16[16,2,2,48,1024]{4,3,2,1,0:T(8,128)(2,1)}), bf16[16,2,2,48,1024]{4,3,2,1,0:T(8,128)(2,1)}, u32[]{:S(2)}, u32[]{:S(2)}) %all-to-all-start) | async-done | bytes 6291488 | tf_op jit(solution)/shard_map/all_to_all | solution.py:331
  147.1 10.8 %all-to-all-start.1 = ((bf16[16,2,2,48,768]{4,3,2,1,0:T(8,128)(2,1)}), bf16[16,2,2,48,768]{4,3,2,1,0:T(8,128)(2,1)}, u32[]{:S(2)}, u32[]{:S(2)}) async-start(bf16[16,2,2,48,768]{4,3,2,1,0:T(8,128)(2,1)} %pack.6), calls=%async_computation.1 | async-start | bytes 9437184 | tf_op jit(solution)/shard_map/all_to_all | solution.py:331
  158.0 1.5 collective-permute-start.10
  159.8 1.3 collective-permute-start.9
  164.8 0.7 and_select_fusion.1
  165.5 0.7 fusion.3
  166.4 0.7 multiply_add_fusion
  167.3 0.7 reshape.66.bias_ref
  168.0 41.1 %attend.5 = (bf16[400,1024]{1,0:T(8,128)(2,1)}, bf16[400,1024]{1,0:T(8,128)(2,1)}, bf16[400,1024]{1,0:T(8,128)(2,1)}, bf16[400,1024]{1,0:T(8,128)(2,1)}) custom-call(f32[1,1536]{1,0:T(1,128)} %reshape.66.bias_ref, bf16[16,2,96,1024]{3,2,1,0:T(8,128)(2,1)} %bitcast.6.kc_ref.vc_ref, bf16[16,2,96,1024]{3,2,1,0:T(8,128)(2,1)} %bitcast.6.kc_ref.vc_ref, ...), custom_call_target="tpu_custom_call" | custom-call | flops 28991029248 | bytes 15728640 | tf_op jit(solution)/shard_map/attend/pallas_call | solution.py:212
  209.2 0.8 collective-permute-start.6
  210.0 1.7 collective-permute-done.9.refs_2_.refs_0_
  211.7 0.7 collective-permute-start.7
  212.5 5.8 %pack.5 = bf16[16,2,2,48,512]{4,3,2,1,0:T(8,128)(2,1)} custom-call(s32[2]{0:T(128)} %pad_add_fusion.place_ref, s32[8,16]{1,0:T(8,128)} %slots_ref.7, s32[8]{0:T(128)} %videos_ref.7, bf16[16,2,48,5120]{3,2,1,0:T(8,128)(2,1)} %cache_ref.7), custom_call_target="tpu_custom_call" | custom-call | bytes 6291456 | tf_op jit(solution)/shard_map/pack/pallas_call | solution.py:62
  218.3 12.2 %collective-permute-done.6.refs_2_ = bf16[400,1024]{1,0:T(8,128)(2,1)} collective-permute-done((bf16[400,1024]{1,0:T(8,128)(2,1)}, bf16[400,1024]{1,0:T(8,128)(2,1)}, u32[]{:S(2)}, u32[]{:S(2)}) %collective-permute-start.6) | collective-permute-done | bytes 819232 | tf_op jit(solution)/shard_map/ppermute | solution.py:321
  230.6 16.6 %collective-permute-done.7.refs_3_ = bf16[400,1024]{1,0:T(8,128)(2,1)} collective-permute-done((bf16[400,1024]{1,0:T(8,128)(2,1)}, bf16[400,1024]{1,0:T(8,128)(2,1)}, u32[]{:S(2)}, u32[]{:S(2)}) %collective-permute-start.7) | collective-permute-done | bytes 819232 | tf_op jit(solution)/shard_map/ppermute | solution.py:321
  247.2 11.0 %all-to-all-done.1 = bf16[16,2,2,48,768]{4,3,2,1,0:T(8,128)(2,1)} async-done(((bf16[16,2,2,48,768]{4,3,2,1,0:T(8,128)(2,1)}), bf16[16,2,2,48,768]{4,3,2,1,0:T(8,128)(2,1)}, u32[]{:S(2)}, u32[]{:S(2)}) %all-to-all-start.1) | async-done | bytes 4718624 | tf_op jit(solution)/shard_map/all_to_all | solution.py:331
  258.2 8.5 %all-to-all-start.2 = ((bf16[16,2,2,48,512]{4,3,2,1,0:T(8,128)(2,1)}), bf16[16,2,2,48,512]{4,3,2,1,0:T(8,128)(2,1)S(1)}, u32[]{:S(2)}, u32[]{:S(2)}) async-start(bf16[16,2,2,48,512]{4,3,2,1,0:T(8,128)(2,1)} %pack.5), calls=%async_computation.2 | async-start | bytes 6291456 | tf_op jit(solution)/shard_map/all_to_all | solution.py:331
  266.7 31.3 %attend.6 = (bf16[400,768]{1,0:T(8,128)(2,1)}, bf16[400,768]{1,0:T(8,128)(2,1)}, bf16[400,768]{1,0:T(8,128)(2,1)}, bf16[400,768]{1,0:T(8,128)(2,1)}) custom-call(f32[1,1536]{1,0:T(1,128)} %reshape.66.bias_ref, bf16[16,2,96,768]{3,2,1,0:T(8,128)(2,1)} %bitcast.9.kc_ref.vc_ref, bf16[16,2,96,768]{3,2,1,0:T(8,128)(2,1)} %bitcast.9.kc_ref.vc_ref, ...), custom_call_target="tpu_custom_call" | custom-call | flops 21743271936 | bytes 11796480 | tf_op jit(solution)/shard_map/attend/pallas_call | solution.py:212
  298.5 1.5 collective-permute-start.12
  300.0 5.2 %pack.4 = bf16[16,2,2,48,256]{4,3,2,1,0:T(8,128)(2,1)} custom-call(s32[2]{0:T(128)} %pad_add_fusion.place_ref, s32[8,16]{1,0:T(8,128)} %slots_ref.7, s32[8]{0:T(128)} %videos_ref.7, bf16[16,2,48,5120]{3,2,1,0:T(8,128)(2,1)} %cache_ref.7), custom_call_target="tpu_custom_call" | custom-call | bytes 3145728 | tf_op jit(solution)/shard_map/pack/pallas_call | solution.py:62
  305.2 5.5 %merge.4.refs_4_ = bf16[384,5120]{1,0:T(8,128)(2,1)} custom-call(s32[2]{0:T(128)} %pad_add_fusion.place_ref, bf16[400,1024]{1,0:T(8,128)(2,1)} %get-tuple-element.38.refs_0_, bf16[400,1024]{1,0:T(8,128)(2,1)} %collective-permute-done.5.refs_1_, bf16[400,1024]{1,0:T(8,128)(2,1)} %collective-permute-done.6.refs_2_, ...), custom_call_target="tpu_custom_call" | custom-call | flops 12582912 | bytes 6291456 | tf_op jit(solution)/shard_map/merge/pallas_call | solution.py:273
  310.7 4.7 %collective-permute-done.12.refs_2_ = bf16[400,768]{1,0:T(8,128)(2,1)S(1)} collective-permute-done((bf16[400,768]{1,0:T(8,128)(2,1)}, bf16[400,768]{1,0:T(8,128)(2,1)S(1)}, u32[]{:S(2)}, u32[]{:S(2)}) %collective-permute-start.12) | collective-permute-done | bytes 614432 | tf_op jit(solution)/shard_map/ppermute | solution.py:321
  315.4 0.8 copy-done.6
  316.2 10.8 %collective-permute-done.13.refs_3_ = bf16[400,768]{1,0:T(8,128)(2,1)} collective-permute-done((bf16[400,768]{1,0:T(8,128)(2,1)}, bf16[400,768]{1,0:T(8,128)(2,1)}, u32[]{:S(2)}, u32[]{:S(2)}) %collective-permute-start.13) | collective-permute-done | bytes 614432 | tf_op jit(solution)/shard_map/ppermute | solution.py:321
  327.0 8.4 %all-to-all-done.2 = bf16[16,2,2,48,512]{4,3,2,1,0:T(8,128)(2,1)S(1)} async-done(((bf16[16,2,2,48,512]{4,3,2,1,0:T(8,128)(2,1)}), bf16[16,2,2,48,512]{4,3,2,1,0:T(8,128)(2,1)S(1)}, u32[]{:S(2)}, u32[]{:S(2)}) %all-to-all-start.2) | async-done | bytes 3145760 | tf_op jit(solution)/shard_map/all_to_all | solution.py:331
  335.4 6.4 %all-to-all-start.3 = ((bf16[16,2,2,48,256]{4,3,2,1,0:T(8,128)(2,1)}), bf16[16,2,2,48,256]{4,3,2,1,0:T(8,128)(2,1)}, u32[]{:S(2)}, u32[]{:S(2)}) async-start(bf16[16,2,2,48,256]{4,3,2,1,0:T(8,128)(2,1)} %pack.4), calls=%async_computation.3 | async-start | bytes 3145728 | tf_op jit(solution)/shard_map/all_to_all | solution.py:331
  341.8 21.6 %attend.9 = (bf16[400,512]{1,0:T(8,128)(2,1)}, bf16[400,512]{1,0:T(8,128)(2,1)}, bf16[400,512]{1,0:T(8,128)(2,1)}, bf16[400,512]{1,0:T(8,128)(2,1)}) custom-call(f32[1,1536]{1,0:T(1,128)} %reshape.66.bias_ref, bf16[16,2,96,512]{3,2,1,0:T(8,128)(2,1)} %bitcast.25, bf16[16,2,96,512]{3,2,1,0:T(8,128)(2,1)} %bitcast.26, bf16[384,1536]{1,0:T(8,128)(2,1)} %copy-done.3, ...), custom_call_target="tpu_custom_call" | custom-call | flops 14495514624 | bytes 7864320 | tf_op jit(solution)/shard_map/attend/pallas_call | solution.py:212
  363.8 1.5 collective-permute-start.18
  365.4 4.4 %merge.5.refs_4_ = bf16[384,5120]{1,0:T(8,128)(2,1)} custom-call(s32[2]{0:T(128)} %pad_add_fusion.place_ref, bf16[400,768]{1,0:T(8,128)(2,1)} %get-tuple-element.43.refs_0_, bf16[400,768]{1,0:T(8,128)(2,1)} %copy-done.5, bf16[400,768]{1,0:T(8,128)(2,1)} %copy-done.6, ...), custom_call_target="tpu_custom_call", output_to_operand_aliasing={{}: (5, {})} | custom-call | flops 9437184 | bytes 4718592 | tf_op jit(solution)/shard_map/merge/pallas_call | solution.py:273
  369.8 9.1 %all-to-all-done.3 = bf16[16,2,2,48,256]{4,3,2,1,0:T(8,128)(2,1)} async-done(((bf16[16,2,2,48,256]{4,3,2,1,0:T(8,128)(2,1)}), bf16[16,2,2,48,256]{4,3,2,1,0:T(8,128)(2,1)}, u32[]{:S(2)}, u32[]{:S(2)}) %all-to-all-start.3) | async-done | bytes 1572896 | tf_op jit(solution)/shard_map/all_to_all | solution.py:331
  378.9 7.2 %attend.8 = (bf16[400,256]{1,0:T(8,128)(2,1)}, bf16[400,256]{1,0:T(8,128)(2,1)}) custom-call(f32[1,1536]{1,0:T(1,128)} %reshape.66.bias_ref, bf16[16,2,96,256]{3,2,1,0:T(8,128)(2,1)} %bitcast.11.kc_ref.vc_ref, bf16[16,2,96,256]{3,2,1,0:T(8,128)(2,1)} %bitcast.11.kc_ref.vc_ref, bf16[384,1536]{1,0:T(8,128)(2,1)} %collective-permute-done.9.refs_2_.refs_0_, ...), custom_call_target="tpu_custom_call" | custom-call | flops 3623878656 | bytes 3145728 | tf_op jit(solution)/shard_map/attend/pallas_call | solution.py:212
  386.1 1.5 collective-permute-start.15
  387.6 7.2 %attend.7 = (bf16[400,256]{1,0:T(8,128)(2,1)}, bf16[400,256]{1,0:T(8,128)(2,1)}) custom-call(f32[1,1536]{1,0:T(1,128)} %reshape.66.bias_ref, bf16[16,2,96,256]{3,2,1,0:T(8,128)(2,1)} %bitcast.11.kc_ref.vc_ref, bf16[16,2,96,256]{3,2,1,0:T(8,128)(2,1)} %bitcast.11.kc_ref.vc_ref, bf16[384,1536]{1,0:T(8,128)(2,1)} %copy-done.3, ...), custom_call_target="tpu_custom_call" | custom-call | flops 3623878656 | bytes 3145728 | tf_op jit(solution)/shard_map/attend/pallas_call | solution.py:212
  394.8 0.7 collective-permute-start.14
  395.5 0.7 copy-done.8
  396.4 3.7 merge.6.refs_4_
  400.2 0.6 copy-done.10
  401.0 3.2 merge.7
  (66 shorter events, 5.2 us)
Async XLA Ops:
  7.6 139.4 %all-to-all-start = ((bf16[16,2,2,48,1024]{4,3,2,1,0:T(8,128)(2,1)}), bf16[16,2,2,48,1024]{4,3,2,1,0:T(8,128)(2,1)}, u32[]{:S(2)}, u32[]{:S(2)}) async-start(bf16[16,2,2,48,1024]{4,3,2,1,0:T(8,128)(2,1)} %pack.7), calls=%async_computation | async-start | bytes 12582912 | tf_op jit(solution)/shard_map/all_to_all | solution.py:331
  27.9 37.9 %collective-permute-start.3 = (bf16[384,2560]{1,0:T(8,128)(2,1)}, bf16[384,2560]{1,0:T(8,128)(2,1)}, u32[]{:S(2)}, u32[]{:S(2)}) collective-permute-start(bf16[384,2560]{1,0:T(8,128)(2,1)} %get-tuple-element.33), channel_id=1, source_target_pairs={{0,8},{8,0},{16,24},{24,16},{1,9},{9,1},{17,25},{25,17},{2,10},{10... | collective-permute-start | bytes 5898248 | tf_op jit(solution)/shard_map/ppermute | solution.py:321
  28.3 38.4 %collective-permute-start.4 = (bf16[384,2560]{1,0:T(8,128)(2,1)}, bf16[384,2560]{1,0:T(8,128)(2,1)}, u32[]{:S(2)}, u32[]{:S(2)}) collective-permute-start(bf16[384,2560]{1,0:T(8,128)(2,1)} %get-tuple-element.34), channel_id=1, source_target_pairs={{0,8},{8,0},{16,24},{24,16},{1,9},{9,1},{17,25},{25,17},{2,10},{10... | collective-permute-start | bytes 5898248 | tf_op jit(solution)/shard_map/ppermute | solution.py:321
  29.6 9.9 %copy-start.4 = (bf16[384,1024]{1,0:T(8,128)(2,1)}, bf16[384,1024]{1,0:T(8,128)(2,1)S(1)}, u32[]{:S(2)}) copy-start(bf16[384,1024]{1,0:T(8,128)(2,1)S(1)} %slice.16.refs_0_) | copy-start | bytes 2359300
  29.6 20.4 %collective-permute-start.1 = (bf16[384,1024]{1,0:T(8,128)(2,1)S(1)}, bf16[384,1024]{1,0:T(8,128)(2,1)S(1)}, u32[]{:S(2)}, u32[]{:S(2)}) collective-permute-start(bf16[384,1024]{1,0:T(8,128)(2,1)S(1)} %slice.16.refs_0_), channel_id=1, source_target_pairs={{0,16},{8,24},{16,0},{24,8},{1,17},{9,25},{17,1},{25,9},{2,18},{10... | collective-permute-start | bytes 2359304 | tf_op jit(solution)/shard_map/ppermute | solution.py:321
  32.4 17.7 %collective-permute-start = (bf16[384,1024]{1,0:T(8,128)(2,1)S(1)}, bf16[384,1024]{1,0:T(8,128)(2,1)S(1)}, u32[]{:S(2)}, u32[]{:S(2)}) collective-permute-start(bf16[384,1024]{1,0:T(8,128)(2,1)S(1)} %slice.17), channel_id=1, source_target_pairs={{0,8},{8,0},{16,24},{24,16},{1,9},{9,1},{17,25},{25,17},{2,10},{10... | collective-permute-start | bytes 2359304 | tf_op jit(solution)/shard_map/ppermute | solution.py:321
  32.5 33.3 %collective-permute-start.2 = (bf16[384,1024]{1,0:T(8,128)(2,1)S(1)}, bf16[384,1024]{1,0:T(8,128)(2,1)S(1)}, u32[]{:S(2)}, u32[]{:S(2)}) collective-permute-start(bf16[384,1024]{1,0:T(8,128)(2,1)S(1)} %slice.17), channel_id=1, source_target_pairs={{0,24},{8,16},{16,8},{24,0},{1,25},{9,17},{17,9},{25,1},{2,26},{10... | collective-permute-start | bytes 2359304 | tf_op jit(solution)/shard_map/ppermute | solution.py:321
  50.1 15.7 %copy-start.14 = (bf16[384,1024]{1,0:T(8,128)(2,1)}, bf16[384,1024]{1,0:T(8,128)(2,1)S(1)}, u32[]{:S(2)}) copy-start(bf16[384,1024]{1,0:T(8,128)(2,1)S(1)} %collective-permute-done.1.refs_2_) | copy-start | bytes 2359300
  50.1 15.7 %copy-start.15 = (bf16[384,1024]{1,0:T(8,128)(2,1)}, bf16[384,1024]{1,0:T(8,128)(2,1)S(1)}, u32[]{:S(2)}) copy-start(bf16[384,1024]{1,0:T(8,128)(2,1)S(1)} %collective-permute-done.refs_1_) | copy-start | bytes 2359300
  65.8 0.9 copy-start.16
  147.1 10.8 %copy-start.2 = (bf16[384,2560]{1,0:T(8,128)(2,1)S(1)}, bf16[384,2560]{1,0:T(8,128)(2,1)}, u32[]{:S(2)}) copy-start(bf16[384,2560]{1,0:T(8,128)(2,1)} %get-tuple-element.32) | copy-start | bytes 5898244
  147.1 111.1 %all-to-all-start.1 = ((bf16[16,2,2,48,768]{4,3,2,1,0:T(8,128)(2,1)}), bf16[16,2,2,48,768]{4,3,2,1,0:T(8,128)(2,1)}, u32[]{:S(2)}, u32[]{:S(2)}) async-start(bf16[16,2,2,48,768]{4,3,2,1,0:T(8,128)(2,1)} %pack.6), calls=%async_computation.1 | async-start | bytes 9437184 | tf_op jit(solution)/shard_map/all_to_all | solution.py:331
  157.9 1.8 copy-start.1
  157.9 3.2 copy-start.13
  157.9 5.7 %copy-start.17 = (s32[8]{0:T(128)S(1)}, s32[8]{0:T(128)}, u32[]{:S(2)}) copy-start(s32[8]{0:T(128)} %param.9) | copy-start | bytes 100
  158.0 60.3 %collective-permute-start.10 = (bf16[384,1536]{1,0:T(8,128)(2,1)S(1)}, bf16[384,1536]{1,0:T(8,128)(2,1)}, u32[]{:S(2)}, u32[]{:S(2)}) collective-permute-start(bf16[384,1536]{1,0:T(8,128)(2,1)S(1)} %slice.19), channel_id=1, source_target_pairs={{0,24},{8,16},{16,8},{24,0},{1,25},{9,17},{17,9},{25,1},{2,26},{10... | collective-permute-start | bytes 3538952 | tf_op jit(solution)/shard_map/ppermute | solution.py:321
  159.5 58.8 %collective-permute-start.8 = (bf16[384,1536]{1,0:T(8,128)(2,1)S(1)}, bf16[384,1536]{1,0:T(8,128)(2,1)}, u32[]{:S(2)}, u32[]{:S(2)}) collective-permute-start(bf16[384,1536]{1,0:T(8,128)(2,1)S(1)} %slice.19), channel_id=1, source_target_pairs={{0,8},{8,0},{16,24},{24,16},{1,9},{9,1},{17,25},{25,17},{2,10},{10... | collective-permute-start | bytes 3538952 | tf_op jit(solution)/shard_map/ppermute | solution.py:321
  159.7 49.3 %copy-start.3 = (bf16[384,1536]{1,0:T(8,128)(2,1)}, bf16[384,1536]{1,0:T(8,128)(2,1)S(1)}, u32[]{:S(2)}) copy-start(bf16[384,1536]{1,0:T(8,128)(2,1)S(1)} %slice.18.refs_0_) | copy-start | bytes 3538948
  159.8 52.0 %collective-permute-start.9 = (bf16[384,1536]{1,0:T(8,128)(2,1)S(1)}, bf16[384,1536]{1,0:T(8,128)(2,1)}, u32[]{:S(2)}, u32[]{:S(2)}) collective-permute-start(bf16[384,1536]{1,0:T(8,128)(2,1)S(1)} %slice.18.refs_0_), channel_id=1, source_target_pairs={{0,16},{8,24},{16,0},{24,8},{1,17},{9,25},{17,1},{25,9},{2,18},{10... | collective-permute-start | bytes 3538952 | tf_op jit(solution)/shard_map/ppermute | solution.py:321
  209.1 9.2 %collective-permute-start.5 = (bf16[400,1024]{1,0:T(8,128)(2,1)}, bf16[400,1024]{1,0:T(8,128)(2,1)}, u32[]{:S(2)}, u32[]{:S(2)}) collective-permute-start(bf16[400,1024]{1,0:T(8,128)(2,1)} %get-tuple-element.39), channel_id=1, source_target_pairs={{8,0},{0,8},{24,16},{16,24},{9,1},{1,9},{25,17},{17,25},{10,2},{2,... | collective-permute-start | bytes 2457608 | tf_op jit(solution)/shard_map/ppermute | solution.py:321
  209.2 21.4 %collective-permute-start.6 = (bf16[400,1024]{1,0:T(8,128)(2,1)}, bf16[400,1024]{1,0:T(8,128)(2,1)}, u32[]{:S(2)}, u32[]{:S(2)}) collective-permute-start(bf16[400,1024]{1,0:T(8,128)(2,1)} %get-tuple-element.40), channel_id=1, source_target_pairs={{16,0},{24,8},{0,16},{8,24},{17,1},{25,9},{1,17},{9,25},{18,2},{26... | collective-permute-start | bytes 2457608 | tf_op jit(solution)/shard_map/ppermute | solution.py:321
  211.7 35.5 %collective-permute-start.7 = (bf16[400,1024]{1,0:T(8,128)(2,1)}, bf16[400,1024]{1,0:T(8,128)(2,1)}, u32[]{:S(2)}, u32[]{:S(2)}) collective-permute-start(bf16[400,1024]{1,0:T(8,128)(2,1)} %get-tuple-element.41), channel_id=1, source_target_pairs={{24,0},{16,8},{8,16},{0,24},{25,1},{17,9},{9,17},{1,25},{26,2},{18... | collective-permute-start | bytes 2457608 | tf_op jit(solution)/shard_map/ppermute | solution.py:321
  258.2 77.2 %all-to-all-start.2 = ((bf16[16,2,2,48,512]{4,3,2,1,0:T(8,128)(2,1)}), bf16[16,2,2,48,512]{4,3,2,1,0:T(8,128)(2,1)S(1)}, u32[]{:S(2)}, u32[]{:S(2)}) async-start(bf16[16,2,2,48,512]{4,3,2,1,0:T(8,128)(2,1)} %pack.5), calls=%async_computation.2 | async-start | bytes 6291456 | tf_op jit(solution)/shard_map/all_to_all | solution.py:331
  298.0 12.7 %collective-permute-start.11 = (bf16[400,768]{1,0:T(8,128)(2,1)}, bf16[400,768]{1,0:T(8,128)(2,1)S(1)}, u32[]{:S(2)}, u32[]{:S(2)}) collective-permute-start(bf16[400,768]{1,0:T(8,128)(2,1)} %get-tuple-element.44), channel_id=1, source_target_pairs={{8,0},{0,8},{24,16},{16,24},{9,1},{1,9},{25,17},{17,25},{10,2},{2,... | collective-permute-start | bytes 1843208 | tf_op jit(solution)/shard_map/ppermute | solution.py:321
  298.5 16.9 %collective-permute-start.12 = (bf16[400,768]{1,0:T(8,128)(2,1)}, bf16[400,768]{1,0:T(8,128)(2,1)S(1)}, u32[]{:S(2)}, u32[]{:S(2)}) collective-permute-start(bf16[400,768]{1,0:T(8,128)(2,1)} %get-tuple-element.45), channel_id=1, source_target_pairs={{16,0},{24,8},{0,16},{8,24},{17,1},{25,9},{1,17},{9,25},{18,2},{26... | collective-permute-start | bytes 1843208 | tf_op jit(solution)/shard_map/ppermute | solution.py:321
  300.0 27.0 %collective-permute-start.13 = (bf16[400,768]{1,0:T(8,128)(2,1)}, bf16[400,768]{1,0:T(8,128)(2,1)}, u32[]{:S(2)}, u32[]{:S(2)}) collective-permute-start(bf16[400,768]{1,0:T(8,128)(2,1)} %get-tuple-element.46), channel_id=1, source_target_pairs={{24,0},{16,8},{8,16},{0,24},{25,1},{17,9},{9,17},{1,25},{26,2},{18... | collective-permute-start | bytes 1843208 | tf_op jit(solution)/shard_map/ppermute | solution.py:321
  310.7 4.7 %copy-start.5 = (bf16[400,768]{1,0:T(8,128)(2,1)}, bf16[400,768]{1,0:T(8,128)(2,1)S(1)}, u32[]{:S(2)}) copy-start(bf16[400,768]{1,0:T(8,128)(2,1)S(1)} %collective-permute-done.11.refs_1_) | copy-start | bytes 1843204
  315.4 0.8 copy-start.6
  335.4 6.5 %copy-start = (bf16[16,2,2,48,512]{4,3,2,1,0:T(8,128)(2,1)}, bf16[16,2,2,48,512]{4,3,2,1,0:T(8,128)(2,1)S(1)}, u32[]{:S(2)}) copy-start(bf16[16,2,2,48,512]{4,3,2,1,0:T(8,128)(2,1)S(1)} %all-to-all-done.2) | copy-start | bytes 9437188
  335.4 43.5 %all-to-all-start.3 = ((bf16[16,2,2,48,256]{4,3,2,1,0:T(8,128)(2,1)}), bf16[16,2,2,48,256]{4,3,2,1,0:T(8,128)(2,1)}, u32[]{:S(2)}, u32[]{:S(2)}) async-start(bf16[16,2,2,48,256]{4,3,2,1,0:T(8,128)(2,1)} %pack.4), calls=%async_computation.3 | async-start | bytes 3145728 | tf_op jit(solution)/shard_map/all_to_all | solution.py:331
  363.4 31.3 %collective-permute-start.17 = (bf16[400,512]{1,0:T(8,128)(2,1)}, bf16[400,512]{1,0:T(8,128)(2,1)S(1)}, u32[]{:S(2)}, u32[]{:S(2)}) collective-permute-start(bf16[400,512]{1,0:T(8,128)(2,1)} %get-tuple-element.54), channel_id=1, source_target_pairs={{8,0},{0,8},{24,16},{16,24},{9,1},{1,9},{25,17},{17,25},{10,2},{2,... | collective-permute-start | bytes 1228808 | tf_op jit(solution)/shard_map/ppermute | solution.py:321
  363.8 31.6 %collective-permute-start.18 = (bf16[400,512]{1,0:T(8,128)(2,1)}, bf16[400,512]{1,0:T(8,128)(2,1)S(1)}, u32[]{:S(2)}, u32[]{:S(2)}) collective-permute-start(bf16[400,512]{1,0:T(8,128)(2,1)} %get-tuple-element.55), channel_id=1, source_target_pairs={{16,0},{24,8},{0,16},{8,24},{17,1},{25,9},{1,17},{9,25},{18,2},{26... | collective-permute-start | bytes 1228808 | tf_op jit(solution)/shard_map/ppermute | solution.py:321
  365.3 30.2 %collective-permute-start.19 = (bf16[400,512]{1,0:T(8,128)(2,1)}, bf16[400,512]{1,0:T(8,128)(2,1)S(1)}, u32[]{:S(2)}, u32[]{:S(2)}) collective-permute-start(bf16[400,512]{1,0:T(8,128)(2,1)} %get-tuple-element.56), channel_id=1, source_target_pairs={{24,0},{16,8},{8,16},{0,24},{25,1},{17,9},{9,17},{1,25},{26,2},{18... | collective-permute-start | bytes 1228808 | tf_op jit(solution)/shard_map/ppermute | solution.py:321
  386.1 14.1 %collective-permute-start.15 = (bf16[400,256]{1,0:T(8,128)(2,1)}, bf16[400,256]{1,0:T(8,128)(2,1)S(1)}, u32[]{:S(2)}, u32[]{:S(2)}) collective-permute-start(bf16[400,256]{1,0:T(8,128)(2,1)} %get-tuple-element.51), channel_id=1, source_target_pairs={{16,0},{24,8},{0,16},{8,24},{17,1},{25,9},{1,17},{9,25},{18,2},{26... | collective-permute-start | bytes 614408 | tf_op jit(solution)/shard_map/ppermute | solution.py:321
  387.6 12.6 %collective-permute-start.16 = (bf16[400,256]{1,0:T(8,128)(2,1)}, bf16[400,256]{1,0:T(8,128)(2,1)S(1)}, u32[]{:S(2)}, u32[]{:S(2)}) collective-permute-start(bf16[400,256]{1,0:T(8,128)(2,1)} %get-tuple-element.52), channel_id=1, source_target_pairs={{24,0},{16,8},{8,16},{0,24},{25,1},{17,9},{9,17},{1,25},{26,2},{18... | collective-permute-start | bytes 614408 | tf_op jit(solution)/shard_map/ppermute | solution.py:321
  394.8 0.8 copy-start.7
  394.8 5.5 %collective-permute-start.14 = (bf16[400,256]{1,0:T(8,128)(2,1)}, bf16[400,256]{1,0:T(8,128)(2,1)S(1)}, u32[]{:S(2)}, u32[]{:S(2)}) collective-permute-start(bf16[400,256]{1,0:T(8,128)(2,1)} %get-tuple-element.50), channel_id=1, source_target_pairs={{8,0},{0,8},{24,16},{16,24},{9,1},{1,9},{25,17},{17,25},{10,2},{2,... | collective-permute-start | bytes 614408 | tf_op jit(solution)/shard_map/ppermute | solution.py:321
  395.5 0.8 copy-start.8
  395.5 0.9 copy-start.9
  400.2 0.7 copy-start.10
  400.2 0.8 copy-start.11
  400.2 0.8 copy-start.12
where the time goes:
time: 406 us; the launch traced here: 404 us
  waiting for transfers between devices  181 us (45%)
  Pallas kernels  162 us (40%)
  starting transfers between devices  46.8 us (12%)
  local copies, waits for them, and re-layouts  7.89 us (2%)
    all_to_all x4, waiting for transfers between devices, spread_out(): lax.all_to_all(sent, ('core', 'rep'), split_axis=0, concat_axis=0, tiled=...  109 us
    pallas_call x5, Pallas kernels, attend(): pl.pallas_call(functools.partial(attend_kernel, heads, pieces), out_shape...  108 us
    ppermute x20, waiting for transfers between devices, move(): return lax.ppermute(value, ('x', 'core'), pairs)  72.3 us
    all_to_all x4, starting transfers between devices, spread_out(): lax.all_to_all(sent, ('core', 'rep'), split_axis=0, concat_axis=0, tiled=...  33.2 us
    pallas_call x4, Pallas kernels, pack(): pl.pallas_call(functools.partial(pack_kernel, cap, head0, width, half), o...  24.5 us
    pallas_call x4, Pallas kernels, merge(): pl.pallas_call(functools.partial(merge_kernel, heads, len(parts) // 2, he...  16.8 us
    ppermute x20, starting transfers between devices, move(): return lax.ppermute(value, ('x', 'core'), pairs)  13.6 us
    pallas_call x1, Pallas kernels, norm(): pl.pallas_call(functools.partial(norm_kernel, half), out_shape=[out] * 6,...  12.8 us
  transfers between devices with their start and end apart: 24, of which 11 were waited for; matrix products, arithmetic and copies ran while one was open for 2% of the time, Pallas kernels for 38%

commit v1 on v0

--- a/solution.py
+++ b/solution.py
@@ -20,9 +20,9 @@
         video = videos_ref[group]
 
         def each_block(block, rank):
-            slot = slots_ref[video, block]
-            mine = slot // slots_dev == own_group
-            pl.when(mine)(functools.partial(visit, group, rank, slot - own_group * slots_dev))
+            slot = slots_ref[video, block] - own_group * slots_dev
+            mine = (slot >= 0) & (slot < slots_dev)
+            pl.when(mine)(functools.partial(visit, group, rank, slot))
             return rank + mine.astype(jnp.int32)
 
         lax.fori_loop(0, slots_ref.shape[1], each_block, jnp.int32(0), unroll=True)
@@ -31,27 +31,35 @@
     lax.fori_loop(0, videos_ref.shape[0], each_group, jnp.int32(0))
 
 
-def pack_kernel(cap, head0, width, half, place_ref, slots_ref, videos_ref, cache_ref, out_ref, sems):
+def pack_kernel(cap, head0, width, half, place_ref, slots_ref, videos_ref, cache_ref, out_ref, held_ref, in_sems, out_sems):
     groups = videos_ref.shape[0]
 
-    def copy_of(slot, group, rank, core):
+    def copy_in(slot, group, rank, core):
         return pltpu.make_async_copy(
             cache_ref.at[slot, :, :, pl.ds(core * half + head0 * HD, width)],
-            out_ref.at[core * groups + group, :, rank],
-            sems.at[(group * cap + rank) * 2 + core],
+            held_ref.at[core * groups + group, :, rank],
+            in_sems.at[(group * cap + rank) * 2 + core],
         )
+
+    def copy_out(group, core):
+        at = core * groups + group
+        return pltpu.make_async_copy(held_ref.at[at], out_ref.at[at], out_sems.at[at])
 
     def visit(group, rank, slot):
         @pl.when(rank < cap)
         def _():
             for core in range(2):
-                copy_of(slot, group, rank, core).start()
+                copy_in(slot, group, rank, core).start()
 
     own_blocks(place_ref[0], slots_ref, videos_ref, cache_ref.shape[0], visit)
     for group in range(groups):
-        for rank in range(cap):
-            for core in range(2):
-                copy_of(0, group, rank, core).wait()
+        for core in range(2):
+            for rank in range(cap):
+                copy_in(0, group, rank, core).wait()
+            copy_out(group, core).start()
+    for group in range(groups):
+        for core in range(2):
+            copy_out(group, core).wait()
 
 
 def pack(cache, place, slots, videos, cap, head0, heads):
@@ -66,8 +74,12 @@
             num_scalar_prefetch=3,
             grid=(1,),
             in_specs=[pl.BlockSpec(memory_space=pl.ANY)],
-            out_specs=pl.BlockSpec(shape, lambda i, *_: (0, 0, 0, 0, 0)),
-            scratch_shapes=[pltpu.SemaphoreType.DMA((2 * groups * cap,))],
+            out_specs=pl.BlockSpec(memory_space=pl.ANY),
+            scratch_shapes=[
+                pltpu.VMEM(shape, cache.dtype),
+                pltpu.SemaphoreType.DMA((2 * groups * cap,)),
+                pltpu.SemaphoreType.DMA((2 * groups,)),
+            ],
         ),
         compiler_params=pltpu.CompilerParams(vmem_limit_bytes=VMEM_LIMIT),
         cost_estimate=pl.CostEstimate(flops=0, bytes_accessed=4 * math.prod(shape), transcendentals=0),

time: 406 us -> 405 us (level)
    pallas_call x4, Pallas kernels: 24.5 us -> 20 us  [pack(): pl.pallas_call(functools.partial(pack_kernel, cap, head0, width, half), o...]
  transfers between devices with their start and end apart: 24 -> 24, of which waited for: 11 -> 11; matrix products, arithmetic and copies ran while one was open for 2% -> 2% of each run, Pallas kernels for 38% -> 37%
where the time goes in v1:
time: 405 us; the launch traced here: 403 us
  waiting for transfers between devices  185 us (46%)
  Pallas kernels  158 us (39%)
  starting transfers between devices  46.7 us (12%)
  local copies, waits for them, and re-layouts  7.9 us (2%)
    all_to_all x4, waiting for transfers between devices, spread_out(): lax.all_to_all(sent, ('core', 'rep'), split_axis=0, concat_axis=0, tiled=...  109 us
    pallas_call x5, Pallas kernels, attend(): pl.pallas_call(functools.partial(attend_kernel, heads, pieces), out_shape...  108 us
    ppermute x20, waiting for transfers between devices, move(): return lax.ppermute(value, ('x', 'core'), pairs)  76 us
    all_to_all x4, starting transfers between devices, spread_out(): lax.all_to_all(sent, ('core', 'rep'), split_axis=0, concat_axis=0, tiled=...  33.1 us
    pallas_call x4, Pallas kernels, pack(): pl.pallas_call(functools.partial(pack_kernel, cap, head0, width, half), o...  20 us
    pallas_call x4, Pallas kernels, merge(): pl.pallas_call(functools.partial(merge_kernel, heads, len(parts) // 2, he...  16.8 us
    ppermute x20, starting transfers between devices, move(): return lax.ppermute(value, ('x', 'core'), pairs)  13.6 us
    pallas_call x1, Pallas kernels, norm(): pl.pallas_call(functools.partial(norm_kernel, half), out_shape=[out] * 6,...  12.8 us
  transfers between devices with their start and end apart: 24, of which 11 were waited for; matrix products, arithmetic and copies ran while one was open for 2% of the time, Pallas kernels for 37%

profile of v1, /device:TPU:0, one launch (start us, length us, event | category | flops | bytes accessed | tf_op | source)
XLA Modules:
  0.0 403.5 jit_solution(7910852333080644661)
XLA Ops:
  0.6 6.2 %pack.7 = bf16[16,2,2,48,1024]{4,3,2,1,0:T(8,128)(2,1)} custom-call(s32[2]{0:T(128)} %pad_add_fusion.place_ref, s32[8,16]{1,0:T(8,128)} %slots_ref.7, s32[8]{0:T(128)} %videos_ref.7, bf16[16,2,48,5120]{3,2,1,0:T(8,128)(2,1)} %cache_ref.7), custom_call_target="tpu_custom_call" | custom-call | bytes 12582912 | tf_op jit(solution)/shard_map/pack/pallas_call | solution.py:70
  6.8 7.4 %all-to-all-start = ((bf16[16,2,2,48,1024]{4,3,2,1,0:T(8,128)(2,1)}), bf16[16,2,2,48,1024]{4,3,2,1,0:T(8,128)(2,1)}, u32[]{:S(2)}, u32[]{:S(2)}) async-start(bf16[16,2,2,48,1024]{4,3,2,1,0:T(8,128)(2,1)} %pack.7), calls=%async_computation | async-start | bytes 12582912 | tf_op jit(solution)/shard_map/all_to_all | solution.py:343
  14.2 12.8 %norm.1 = (bf16[384,2560]{1,0:T(8,128)(2,1)}, bf16[384,2560]{1,0:T(8,128)(2,1)}, bf16[384,2560]{1,0:T(8,128)(2,1)}, bf16[384,2560]{1,0:T(8,128)(2,1)}, bf16[384,...) custom-call(s32[2]{0:T(128)} %pad_add_fusion.place_ref, bf16[3,384,5120]{2,1,0:T(8,128)(2,1)} %bitcast.24, f32[2,5120]{1,0:T(2,128)} %gains_ref.1), custom_call_target="tpu_custom_call" | custom-call | flops 15728640 | bytes 23592960 | tf_op jit(solution)/shard_map/norm/pallas_call | solution.py:119
  27.6 1.2 slice.16.refs_0_
  28.8 1.6 collective-permute-start.1
  30.3 1.2 slice.17
  32.2 4.9 %pack.6 = bf16[16,2,2,48,768]{4,3,2,1,0:T(8,128)(2,1)} custom-call(s32[2]{0:T(128)} %pad_add_fusion.place_ref, s32[8,16]{1,0:T(8,128)} %slots_ref.7, s32[8]{0:T(128)} %videos_ref.7, bf16[16,2,48,5120]{3,2,1,0:T(8,128)(2,1)} %cache_ref.7), custom_call_target="tpu_custom_call" | custom-call | bytes 9437184 | tf_op jit(solution)/shard_map/pack/pallas_call | solution.py:70
  37.2 12.0 %collective-permute-done.1.refs_2_ = bf16[384,1024]{1,0:T(8,128)(2,1)S(1)} collective-permute-done((bf16[384,1024]{1,0:T(8,128)(2,1)S(1)}, bf16[384,1024]{1,0:T(8,128)(2,1)S(1)}, u32[]{:S(2)}, u32[]{:S(2)}) %collective-permute-start.1) | collective-permute-done | bytes 786464 | tf_op jit(solution)/shard_map/ppermute | solution.py:333
  49.2 15.7 %collective-permute-done.2.refs_3_ = bf16[384,1024]{1,0:T(8,128)(2,1)S(1)} collective-permute-done((bf16[384,1024]{1,0:T(8,128)(2,1)S(1)}, bf16[384,1024]{1,0:T(8,128)(2,1)S(1)}, u32[]{:S(2)}, u32[]{:S(2)}) %collective-permute-start.2) | collective-permute-done | bytes 786464 | tf_op jit(solution)/shard_map/ppermute | solution.py:333
  64.9 0.9 copy-done.16
  65.8 80.4 %all-to-all-done = bf16[16,2,2,48,1024]{4,3,2,1,0:T(8,128)(2,1)} async-done(((bf16[16,2,2,48,1024]{4,3,2,1,0:T(8,128)(2,1)}), bf16[16,2,2,48,1024]{4,3,2,1,0:T(8,128)(2,1)}, u32[]{:S(2)}, u32[]{:S(2)}) %all-to-all-start) | async-done | bytes 6291488 | tf_op jit(solution)/shard_map/all_to_all | solution.py:343
  146.2 10.8 %all-to-all-start.1 = ((bf16[16,2,2,48,768]{4,3,2,1,0:T(8,128)(2,1)}), bf16[16,2,2,48,768]{4,3,2,1,0:T(8,128)(2,1)}, u32[]{:S(2)}, u32[]{:S(2)}) async-start(bf16[16,2,2,48,768]{4,3,2,1,0:T(8,128)(2,1)} %pack.6), calls=%async_computation.1 | async-start | bytes 9437184 | tf_op jit(solution)/shard_map/all_to_all | solution.py:343
  157.1 1.5 collective-permute-start.10
  158.9 1.3 collective-permute-start.9
  164.0 0.7 and_select_fusion.1
  164.7 0.7 fusion.3
  165.6 0.7 multiply_add_fusion
  166.4 0.7 reshape.66.bias_ref
  167.1 41.1 %attend.5 = (bf16[400,1024]{1,0:T(8,128)(2,1)}, bf16[400,1024]{1,0:T(8,128)(2,1)}, bf16[400,1024]{1,0:T(8,128)(2,1)}, bf16[400,1024]{1,0:T(8,128)(2,1)}) custom-call(f32[1,1536]{1,0:T(1,128)} %reshape.66.bias_ref, bf16[16,2,96,1024]{3,2,1,0:T(8,128)(2,1)} %bitcast.6.kc_ref.vc_ref, bf16[16,2,96,1024]{3,2,1,0:T(8,128)(2,1)} %bitcast.6.kc_ref.vc_ref, ...), custom_call_target="tpu_custom_call" | custom-call | flops 28991029248 | bytes 15728640 | tf_op jit(solution)/shard_map/attend/pallas_call | solution.py:224
  208.3 0.8 collective-permute-start.6
  209.1 1.7 collective-permute-done.9.refs_2_.refs_0_
  210.8 0.7 collective-permute-start.7
  211.6 4.6 %pack.5 = bf16[16,2,2,48,512]{4,3,2,1,0:T(8,128)(2,1)} custom-call(s32[2]{0:T(128)} %pad_add_fusion.place_ref, s32[8,16]{1,0:T(8,128)} %slots_ref.7, s32[8]{0:T(128)} %videos_ref.7, bf16[16,2,48,5120]{3,2,1,0:T(8,128)(2,1)} %cache_ref.7), custom_call_target="tpu_custom_call" | custom-call | bytes 6291456 | tf_op jit(solution)/shard_map/pack/pallas_call | solution.py:70
  216.2 13.5 %collective-permute-done.6.refs_2_ = bf16[400,1024]{1,0:T(8,128)(2,1)} collective-permute-done((bf16[400,1024]{1,0:T(8,128)(2,1)}, bf16[400,1024]{1,0:T(8,128)(2,1)}, u32[]{:S(2)}, u32[]{:S(2)}) %collective-permute-start.6) | collective-permute-done | bytes 819232 | tf_op jit(solution)/shard_map/ppermute | solution.py:333
  229.7 16.6 %collective-permute-done.7.refs_3_ = bf16[400,1024]{1,0:T(8,128)(2,1)} collective-permute-done((bf16[400,1024]{1,0:T(8,128)(2,1)}, bf16[400,1024]{1,0:T(8,128)(2,1)}, u32[]{:S(2)}, u32[]{:S(2)}) %collective-permute-start.7) | collective-permute-done | bytes 819232 | tf_op jit(solution)/shard_map/ppermute | solution.py:333
  246.4 11.0 %all-to-all-done.1 = bf16[16,2,2,48,768]{4,3,2,1,0:T(8,128)(2,1)} async-done(((bf16[16,2,2,48,768]{4,3,2,1,0:T(8,128)(2,1)}), bf16[16,2,2,48,768]{4,3,2,1,0:T(8,128)(2,1)}, u32[]{:S(2)}, u32[]{:S(2)}) %all-to-all-start.1) | async-done | bytes 4718624 | tf_op jit(solution)/shard_map/all_to_all | solution.py:343
  257.3 8.5 %all-to-all-start.2 = ((bf16[16,2,2,48,512]{4,3,2,1,0:T(8,128)(2,1)}), bf16[16,2,2,48,512]{4,3,2,1,0:T(8,128)(2,1)S(1)}, u32[]{:S(2)}, u32[]{:S(2)}) async-start(bf16[16,2,2,48,512]{4,3,2,1,0:T(8,128)(2,1)} %pack.5), calls=%async_computation.2 | async-start | bytes 6291456 | tf_op jit(solution)/shard_map/all_to_all | solution.py:343
  265.8 31.3 %attend.6 = (bf16[400,768]{1,0:T(8,128)(2,1)}, bf16[400,768]{1,0:T(8,128)(2,1)}, bf16[400,768]{1,0:T(8,128)(2,1)}, bf16[400,768]{1,0:T(8,128)(2,1)}) custom-call(f32[1,1536]{1,0:T(1,128)} %reshape.66.bias_ref, bf16[16,2,96,768]{3,2,1,0:T(8,128)(2,1)} %bitcast.9.kc_ref.vc_ref, bf16[16,2,96,768]{3,2,1,0:T(8,128)(2,1)} %bitcast.9.kc_ref.vc_ref, ...), custom_call_target="tpu_custom_call" | custom-call | flops 21743271936 | bytes 11796480 | tf_op jit(solution)/shard_map/attend/pallas_call | solution.py:224
  297.6 1.5 collective-permute-start.12
  299.1 4.3 %pack.4 = bf16[16,2,2,48,256]{4,3,2,1,0:T(8,128)(2,1)} custom-call(s32[2]{0:T(128)} %pad_add_fusion.place_ref, s32[8,16]{1,0:T(8,128)} %slots_ref.7, s32[8]{0:T(128)} %videos_ref.7, bf16[16,2,48,5120]{3,2,1,0:T(8,128)(2,1)} %cache_ref.7), custom_call_target="tpu_custom_call" | custom-call | bytes 3145728 | tf_op jit(solution)/shard_map/pack/pallas_call | solution.py:70
  303.4 5.5 %merge.4.refs_4_ = bf16[384,5120]{1,0:T(8,128)(2,1)} custom-call(s32[2]{0:T(128)} %pad_add_fusion.place_ref, bf16[400,1024]{1,0:T(8,128)(2,1)} %get-tuple-element.38.refs_0_, bf16[400,1024]{1,0:T(8,128)(2,1)} %collective-permute-done.5.refs_1_, bf16[400,1024]{1,0:T(8,128)(2,1)} %collective-permute-done.6.refs_2_, ...), custom_call_target="tpu_custom_call" | custom-call | flops 12582912 | bytes 6291456 | tf_op jit(solution)/shard_map/merge/pallas_call | solution.py:285
  308.9 5.6 %collective-permute-done.12.refs_2_ = bf16[400,768]{1,0:T(8,128)(2,1)S(1)} collective-permute-done((bf16[400,768]{1,0:T(8,128)(2,1)}, bf16[400,768]{1,0:T(8,128)(2,1)S(1)}, u32[]{:S(2)}, u32[]{:S(2)}) %collective-permute-start.12) | collective-permute-done | bytes 614432 | tf_op jit(solution)/shard_map/ppermute | solution.py:333
  314.5 0.8 copy-done.6
  315.4 10.8 %collective-permute-done.13.refs_3_ = bf16[400,768]{1,0:T(8,128)(2,1)} collective-permute-done((bf16[400,768]{1,0:T(8,128)(2,1)}, bf16[400,768]{1,0:T(8,128)(2,1)}, u32[]{:S(2)}, u32[]{:S(2)}) %collective-permute-start.13) | collective-permute-done | bytes 614432 | tf_op jit(solution)/shard_map/ppermute | solution.py:333
  326.1 8.4 %all-to-all-done.2 = bf16[16,2,2,48,512]{4,3,2,1,0:T(8,128)(2,1)S(1)} async-done(((bf16[16,2,2,48,512]{4,3,2,1,0:T(8,128)(2,1)}), bf16[16,2,2,48,512]{4,3,2,1,0:T(8,128)(2,1)S(1)}, u32[]{:S(2)}, u32[]{:S(2)}) %all-to-all-start.2) | async-done | bytes 3145760 | tf_op jit(solution)/shard_map/all_to_all | solution.py:343
  334.5 6.4 %all-to-all-start.3 = ((bf16[16,2,2,48,256]{4,3,2,1,0:T(8,128)(2,1)}), bf16[16,2,2,48,256]{4,3,2,1,0:T(8,128)(2,1)}, u32[]{:S(2)}, u32[]{:S(2)}) async-start(bf16[16,2,2,48,256]{4,3,2,1,0:T(8,128)(2,1)} %pack.4), calls=%async_computation.3 | async-start | bytes 3145728 | tf_op jit(solution)/shard_map/all_to_all | solution.py:343
  341.0 21.6 %attend.9 = (bf16[400,512]{1,0:T(8,128)(2,1)}, bf16[400,512]{1,0:T(8,128)(2,1)}, bf16[400,512]{1,0:T(8,128)(2,1)}, bf16[400,512]{1,0:T(8,128)(2,1)}) custom-call(f32[1,1536]{1,0:T(1,128)} %reshape.66.bias_ref, bf16[16,2,96,512]{3,2,1,0:T(8,128)(2,1)} %bitcast.25, bf16[16,2,96,512]{3,2,1,0:T(8,128)(2,1)} %bitcast.26, bf16[384,1536]{1,0:T(8,128)(2,1)} %copy-done.3, ...), custom_call_target="tpu_custom_call" | custom-call | flops 14495514624 | bytes 7864320 | tf_op jit(solution)/shard_map/attend/pallas_call | solution.py:224
  363.0 1.5 collective-permute-start.18
  364.5 4.4 %merge.5.refs_4_ = bf16[384,5120]{1,0:T(8,128)(2,1)} custom-call(s32[2]{0:T(128)} %pad_add_fusion.place_ref, bf16[400,768]{1,0:T(8,128)(2,1)} %get-tuple-element.43.refs_0_, bf16[400,768]{1,0:T(8,128)(2,1)} %copy-done.5, bf16[400,768]{1,0:T(8,128)(2,1)} %copy-done.6, ...), custom_call_target="tpu_custom_call", output_to_operand_aliasing={{}: (5, {})} | custom-call | flops 9437184 | bytes 4718592 | tf_op jit(solution)/shard_map/merge/pallas_call | solution.py:285
  368.9 9.1 %all-to-all-done.3 = bf16[16,2,2,48,256]{4,3,2,1,0:T(8,128)(2,1)} async-done(((bf16[16,2,2,48,256]{4,3,2,1,0:T(8,128)(2,1)}), bf16[16,2,2,48,256]{4,3,2,1,0:T(8,128)(2,1)}, u32[]{:S(2)}, u32[]{:S(2)}) %all-to-all-start.3) | async-done | bytes 1572896 | tf_op jit(solution)/shard_map/all_to_all | solution.py:343
  378.1 7.2 %attend.8 = (bf16[400,256]{1,0:T(8,128)(2,1)}, bf16[400,256]{1,0:T(8,128)(2,1)}) custom-call(f32[1,1536]{1,0:T(1,128)} %reshape.66.bias_ref, bf16[16,2,96,256]{3,2,1,0:T(8,128)(2,1)} %bitcast.11.kc_ref.vc_ref, bf16[16,2,96,256]{3,2,1,0:T(8,128)(2,1)} %bitcast.11.kc_ref.vc_ref, bf16[384,1536]{1,0:T(8,128)(2,1)} %collective-permute-done.9.refs_2_.refs_0_, ...), custom_call_target="tpu_custom_call" | custom-call | flops 3623878656 | bytes 3145728 | tf_op jit(solution)/shard_map/attend/pallas_call | solution.py:224
  385.2 1.5 collective-permute-start.15
  386.7 7.2 %attend.7 = (bf16[400,256]{1,0:T(8,128)(2,1)}, bf16[400,256]{1,0:T(8,128)(2,1)}) custom-call(f32[1,1536]{1,0:T(1,128)} %reshape.66.bias_ref, bf16[16,2,96,256]{3,2,1,0:T(8,128)(2,1)} %bitcast.11.kc_ref.vc_ref, bf16[16,2,96,256]{3,2,1,0:T(8,128)(2,1)} %bitcast.11.kc_ref.vc_ref, bf16[384,1536]{1,0:T(8,128)(2,1)} %copy-done.3, ...), custom_call_target="tpu_custom_call" | custom-call | flops 3623878656 | bytes 3145728 | tf_op jit(solution)/shard_map/attend/pallas_call | solution.py:224
  393.9 0.7 collective-permute-start.14
  394.6 0.7 copy-done.8
  395.5 3.7 merge.6.refs_4_
  399.3 0.6 copy-done.10
  400.1 3.2 merge.7
  (66 shorter events, 5.2 us)
Async XLA Ops:
  6.8 139.4 %all-to-all-start = ((bf16[16,2,2,48,1024]{4,3,2,1,0:T(8,128)(2,1)}), bf16[16,2,2,48,1024]{4,3,2,1,0:T(8,128)(2,1)}, u32[]{:S(2)}, u32[]{:S(2)}) async-start(bf16[16,2,2,48,1024]{4,3,2,1,0:T(8,128)(2,1)} %pack.7), calls=%async_computation | async-start | bytes 12582912 | tf_op jit(solution)/shard_map/all_to_all | solution.py:343
  27.1 37.9 %collective-permute-start.3 = (bf16[384,2560]{1,0:T(8,128)(2,1)}, bf16[384,2560]{1,0:T(8,128)(2,1)}, u32[]{:S(2)}, u32[]{:S(2)}) collective-permute-start(bf16[384,2560]{1,0:T(8,128)(2,1)} %get-tuple-element.33), channel_id=1, source_target_pairs={{0,8},{8,0},{16,24},{24,16},{1,9},{9,1},{17,25},{25,17},{2,10},{10... | collective-permute-start | bytes 5898248 | tf_op jit(solution)/shard_map/ppermute | solution.py:333
  27.4 38.4 %collective-permute-start.4 = (bf16[384,2560]{1,0:T(8,128)(2,1)}, bf16[384,2560]{1,0:T(8,128)(2,1)}, u32[]{:S(2)}, u32[]{:S(2)}) collective-permute-start(bf16[384,2560]{1,0:T(8,128)(2,1)} %get-tuple-element.34), channel_id=1, source_target_pairs={{0,8},{8,0},{16,24},{24,16},{1,9},{9,1},{17,25},{25,17},{2,10},{10... | collective-permute-start | bytes 5898248 | tf_op jit(solution)/shard_map/ppermute | solution.py:333
  28.7 8.4 %copy-start.4 = (bf16[384,1024]{1,0:T(8,128)(2,1)}, bf16[384,1024]{1,0:T(8,128)(2,1)S(1)}, u32[]{:S(2)}) copy-start(bf16[384,1024]{1,0:T(8,128)(2,1)S(1)} %slice.16.refs_0_) | copy-start | bytes 2359300
  28.8 20.4 %collective-permute-start.1 = (bf16[384,1024]{1,0:T(8,128)(2,1)S(1)}, bf16[384,1024]{1,0:T(8,128)(2,1)S(1)}, u32[]{:S(2)}, u32[]{:S(2)}) collective-permute-start(bf16[384,1024]{1,0:T(8,128)(2,1)S(1)} %slice.16.refs_0_), channel_id=1, source_target_pairs={{0,16},{8,24},{16,0},{24,8},{1,17},{9,25},{17,1},{25,9},{2,18},{10... | collective-permute-start | bytes 2359304 | tf_op jit(solution)/shard_map/ppermute | solution.py:333
  31.5 17.7 %collective-permute-start = (bf16[384,1024]{1,0:T(8,128)(2,1)S(1)}, bf16[384,1024]{1,0:T(8,128)(2,1)S(1)}, u32[]{:S(2)}, u32[]{:S(2)}) collective-permute-start(bf16[384,1024]{1,0:T(8,128)(2,1)S(1)} %slice.17), channel_id=1, source_target_pairs={{0,8},{8,0},{16,24},{24,16},{1,9},{9,1},{17,25},{25,17},{2,10},{10... | collective-permute-start | bytes 2359304 | tf_op jit(solution)/shard_map/ppermute | solution.py:333
  31.6 33.3 %collective-permute-start.2 = (bf16[384,1024]{1,0:T(8,128)(2,1)S(1)}, bf16[384,1024]{1,0:T(8,128)(2,1)S(1)}, u32[]{:S(2)}, u32[]{:S(2)}) collective-permute-start(bf16[384,1024]{1,0:T(8,128)(2,1)S(1)} %slice.17), channel_id=1, source_target_pairs={{0,24},{8,16},{16,8},{24,0},{1,25},{9,17},{17,9},{25,1},{2,26},{10... | collective-permute-start | bytes 2359304 | tf_op jit(solution)/shard_map/ppermute | solution.py:333
  49.2 15.7 %copy-start.14 = (bf16[384,1024]{1,0:T(8,128)(2,1)}, bf16[384,1024]{1,0:T(8,128)(2,1)S(1)}, u32[]{:S(2)}) copy-start(bf16[384,1024]{1,0:T(8,128)(2,1)S(1)} %collective-permute-done.1.refs_2_) | copy-start | bytes 2359300
  49.2 15.7 %copy-start.15 = (bf16[384,1024]{1,0:T(8,128)(2,1)}, bf16[384,1024]{1,0:T(8,128)(2,1)S(1)}, u32[]{:S(2)}) copy-start(bf16[384,1024]{1,0:T(8,128)(2,1)S(1)} %collective-permute-done.refs_1_) | copy-start | bytes 2359300
  64.9 0.9 copy-start.16
  146.2 10.8 %copy-start.2 = (bf16[384,2560]{1,0:T(8,128)(2,1)S(1)}, bf16[384,2560]{1,0:T(8,128)(2,1)}, u32[]{:S(2)}) copy-start(bf16[384,2560]{1,0:T(8,128)(2,1)} %get-tuple-element.32) | copy-start | bytes 5898244
  146.2 111.1 %all-to-all-start.1 = ((bf16[16,2,2,48,768]{4,3,2,1,0:T(8,128)(2,1)}), bf16[16,2,2,48,768]{4,3,2,1,0:T(8,128)(2,1)}, u32[]{:S(2)}, u32[]{:S(2)}) async-start(bf16[16,2,2,48,768]{4,3,2,1,0:T(8,128)(2,1)} %pack.6), calls=%async_computation.1 | async-start | bytes 9437184 | tf_op jit(solution)/shard_map/all_to_all | solution.py:343
  157.0 1.8 copy-start.1
  157.0 3.2 copy-start.13
  157.0 5.7 %copy-start.17 = (s32[8]{0:T(128)S(1)}, s32[8]{0:T(128)}, u32[]{:S(2)}) copy-start(s32[8]{0:T(128)} %param.9) | copy-start | bytes 100
  157.1 59.1 %collective-permute-start.10 = (bf16[384,1536]{1,0:T(8,128)(2,1)S(1)}, bf16[384,1536]{1,0:T(8,128)(2,1)}, u32[]{:S(2)}, u32[]{:S(2)}) collective-permute-start(bf16[384,1536]{1,0:T(8,128)(2,1)S(1)} %slice.19), channel_id=1, source_target_pairs={{0,24},{8,16},{16,8},{24,0},{1,25},{9,17},{17,9},{25,1},{2,26},{10... | collective-permute-start | bytes 3538952 | tf_op jit(solution)/shard_map/ppermute | solution.py:333
  158.6 57.6 %collective-permute-start.8 = (bf16[384,1536]{1,0:T(8,128)(2,1)S(1)}, bf16[384,1536]{1,0:T(8,128)(2,1)}, u32[]{:S(2)}, u32[]{:S(2)}) collective-permute-start(bf16[384,1536]{1,0:T(8,128)(2,1)S(1)} %slice.19), channel_id=1, source_target_pairs={{0,8},{8,0},{16,24},{24,16},{1,9},{9,1},{17,25},{25,17},{2,10},{10... | collective-permute-start | bytes 3538952 | tf_op jit(solution)/shard_map/ppermute | solution.py:333
  158.9 49.3 %copy-start.3 = (bf16[384,1536]{1,0:T(8,128)(2,1)}, bf16[384,1536]{1,0:T(8,128)(2,1)S(1)}, u32[]{:S(2)}) copy-start(bf16[384,1536]{1,0:T(8,128)(2,1)S(1)} %slice.18.refs_0_) | copy-start | bytes 3538948
  158.9 52.0 %collective-permute-start.9 = (bf16[384,1536]{1,0:T(8,128)(2,1)S(1)}, bf16[384,1536]{1,0:T(8,128)(2,1)}, u32[]{:S(2)}, u32[]{:S(2)}) collective-permute-start(bf16[384,1536]{1,0:T(8,128)(2,1)S(1)} %slice.18.refs_0_), channel_id=1, source_target_pairs={{0,16},{8,24},{16,0},{24,8},{1,17},{9,25},{17,1},{25,9},{2,18},{10... | collective-permute-start | bytes 3538952 | tf_op jit(solution)/shard_map/ppermute | solution.py:333
  208.2 8.0 %collective-permute-start.5 = (bf16[400,1024]{1,0:T(8,128)(2,1)}, bf16[400,1024]{1,0:T(8,128)(2,1)}, u32[]{:S(2)}, u32[]{:S(2)}) collective-permute-start(bf16[400,1024]{1,0:T(8,128)(2,1)} %get-tuple-element.39), channel_id=1, source_target_pairs={{8,0},{0,8},{24,16},{16,24},{9,1},{1,9},{25,17},{17,25},{10,2},{2,... | collective-permute-start | bytes 2457608 | tf_op jit(solution)/shard_map/ppermute | solution.py:333
  208.3 21.4 %collective-permute-start.6 = (bf16[400,1024]{1,0:T(8,128)(2,1)}, bf16[400,1024]{1,0:T(8,128)(2,1)}, u32[]{:S(2)}, u32[]{:S(2)}) collective-permute-start(bf16[400,1024]{1,0:T(8,128)(2,1)} %get-tuple-element.40), channel_id=1, source_target_pairs={{16,0},{24,8},{0,16},{8,24},{17,1},{25,9},{1,17},{9,25},{18,2},{26... | collective-permute-start | bytes 2457608 | tf_op jit(solution)/shard_map/ppermute | solution.py:333
  210.8 35.5 %collective-permute-start.7 = (bf16[400,1024]{1,0:T(8,128)(2,1)}, bf16[400,1024]{1,0:T(8,128)(2,1)}, u32[]{:S(2)}, u32[]{:S(2)}) collective-permute-start(bf16[400,1024]{1,0:T(8,128)(2,1)} %get-tuple-element.41), channel_id=1, source_target_pairs={{24,0},{16,8},{8,16},{0,24},{25,1},{17,9},{9,17},{1,25},{26,2},{18... | collective-permute-start | bytes 2457608 | tf_op jit(solution)/shard_map/ppermute | solution.py:333
  257.3 77.2 %all-to-all-start.2 = ((bf16[16,2,2,48,512]{4,3,2,1,0:T(8,128)(2,1)}), bf16[16,2,2,48,512]{4,3,2,1,0:T(8,128)(2,1)S(1)}, u32[]{:S(2)}, u32[]{:S(2)}) async-start(bf16[16,2,2,48,512]{4,3,2,1,0:T(8,128)(2,1)} %pack.5), calls=%async_computation.2 | async-start | bytes 6291456 | tf_op jit(solution)/shard_map/all_to_all | solution.py:343
  297.1 11.8 %collective-permute-start.11 = (bf16[400,768]{1,0:T(8,128)(2,1)}, bf16[400,768]{1,0:T(8,128)(2,1)S(1)}, u32[]{:S(2)}, u32[]{:S(2)}) collective-permute-start(bf16[400,768]{1,0:T(8,128)(2,1)} %get-tuple-element.44), channel_id=1, source_target_pairs={{8,0},{0,8},{24,16},{16,24},{9,1},{1,9},{25,17},{17,25},{10,2},{2,... | collective-permute-start | bytes 1843208 | tf_op jit(solution)/shard_map/ppermute | solution.py:333
  297.6 16.9 %collective-permute-start.12 = (bf16[400,768]{1,0:T(8,128)(2,1)}, bf16[400,768]{1,0:T(8,128)(2,1)S(1)}, u32[]{:S(2)}, u32[]{:S(2)}) collective-permute-start(bf16[400,768]{1,0:T(8,128)(2,1)} %get-tuple-element.45), channel_id=1, source_target_pairs={{16,0},{24,8},{0,16},{8,24},{17,1},{25,9},{1,17},{9,25},{18,2},{26... | collective-permute-start | bytes 1843208 | tf_op jit(solution)/shard_map/ppermute | solution.py:333
  299.1 27.0 %collective-permute-start.13 = (bf16[400,768]{1,0:T(8,128)(2,1)}, bf16[400,768]{1,0:T(8,128)(2,1)}, u32[]{:S(2)}, u32[]{:S(2)}) collective-permute-start(bf16[400,768]{1,0:T(8,128)(2,1)} %get-tuple-element.46), channel_id=1, source_target_pairs={{24,0},{16,8},{8,16},{0,24},{25,1},{17,9},{9,17},{1,25},{26,2},{18... | collective-permute-start | bytes 1843208 | tf_op jit(solution)/shard_map/ppermute | solution.py:333
  308.9 5.6 %copy-start.5 = (bf16[400,768]{1,0:T(8,128)(2,1)}, bf16[400,768]{1,0:T(8,128)(2,1)S(1)}, u32[]{:S(2)}) copy-start(bf16[400,768]{1,0:T(8,128)(2,1)S(1)} %collective-permute-done.11.refs_1_) | copy-start | bytes 1843204
  314.5 0.8 copy-start.6
  334.5 6.5 %copy-start = (bf16[16,2,2,48,512]{4,3,2,1,0:T(8,128)(2,1)}, bf16[16,2,2,48,512]{4,3,2,1,0:T(8,128)(2,1)S(1)}, u32[]{:S(2)}) copy-start(bf16[16,2,2,48,512]{4,3,2,1,0:T(8,128)(2,1)S(1)} %all-to-all-done.2) | copy-start | bytes 9437188
  334.5 43.5 %all-to-all-start.3 = ((bf16[16,2,2,48,256]{4,3,2,1,0:T(8,128)(2,1)}), bf16[16,2,2,48,256]{4,3,2,1,0:T(8,128)(2,1)}, u32[]{:S(2)}, u32[]{:S(2)}) async-start(bf16[16,2,2,48,256]{4,3,2,1,0:T(8,128)(2,1)} %pack.4), calls=%async_computation.3 | async-start | bytes 3145728 | tf_op jit(solution)/shard_map/all_to_all | solution.py:343
  362.6 31.3 %collective-permute-start.17 = (bf16[400,512]{1,0:T(8,128)(2,1)}, bf16[400,512]{1,0:T(8,128)(2,1)S(1)}, u32[]{:S(2)}, u32[]{:S(2)}) collective-permute-start(bf16[400,512]{1,0:T(8,128)(2,1)} %get-tuple-element.54), channel_id=1, source_target_pairs={{8,0},{0,8},{24,16},{16,24},{9,1},{1,9},{25,17},{17,25},{10,2},{2,... | collective-permute-start | bytes 1228808 | tf_op jit(solution)/shard_map/ppermute | solution.py:333
  363.0 31.6 %collective-permute-start.18 = (bf16[400,512]{1,0:T(8,128)(2,1)}, bf16[400,512]{1,0:T(8,128)(2,1)S(1)}, u32[]{:S(2)}, u32[]{:S(2)}) collective-permute-start(bf16[400,512]{1,0:T(8,128)(2,1)} %get-tuple-element.55), channel_id=1, source_target_pairs={{16,0},{24,8},{0,16},{8,24},{17,1},{25,9},{1,17},{9,25},{18,2},{26... | collective-permute-start | bytes 1228808 | tf_op jit(solution)/shard_map/ppermute | solution.py:333
  364.5 30.1 %collective-permute-start.19 = (bf16[400,512]{1,0:T(8,128)(2,1)}, bf16[400,512]{1,0:T(8,128)(2,1)S(1)}, u32[]{:S(2)}, u32[]{:S(2)}) collective-permute-start(bf16[400,512]{1,0:T(8,128)(2,1)} %get-tuple-element.56), channel_id=1, source_target_pairs={{24,0},{16,8},{8,16},{0,24},{25,1},{17,9},{9,17},{1,25},{26,2},{18... | collective-permute-start | bytes 1228808 | tf_op jit(solution)/shard_map/ppermute | solution.py:333
  385.2 14.1 %collective-permute-start.15 = (bf16[400,256]{1,0:T(8,128)(2,1)}, bf16[400,256]{1,0:T(8,128)(2,1)S(1)}, u32[]{:S(2)}, u32[]{:S(2)}) collective-permute-start(bf16[400,256]{1,0:T(8,128)(2,1)} %get-tuple-element.51), channel_id=1, source_target_pairs={{16,0},{24,8},{0,16},{8,24},{17,1},{25,9},{1,17},{9,25},{18,2},{26... | collective-permute-start | bytes 614408 | tf_op jit(solution)/shard_map/ppermute | solution.py:333
  386.7 12.6 %collective-permute-start.16 = (bf16[400,256]{1,0:T(8,128)(2,1)}, bf16[400,256]{1,0:T(8,128)(2,1)S(1)}, u32[]{:S(2)}, u32[]{:S(2)}) collective-permute-start(bf16[400,256]{1,0:T(8,128)(2,1)} %get-tuple-element.52), channel_id=1, source_target_pairs={{24,0},{16,8},{8,16},{0,24},{25,1},{17,9},{9,17},{1,25},{26,2},{18... | collective-permute-start | bytes 614408 | tf_op jit(solution)/shard_map/ppermute | solution.py:333
  393.9 0.8 copy-start.7
  393.9 5.4 %collective-permute-start.14 = (bf16[400,256]{1,0:T(8,128)(2,1)}, bf16[400,256]{1,0:T(8,128)(2,1)S(1)}, u32[]{:S(2)}, u32[]{:S(2)}) collective-permute-start(bf16[400,256]{1,0:T(8,128)(2,1)} %get-tuple-element.50), channel_id=1, source_target_pairs={{8,0},{0,8},{24,16},{16,24},{9,1},{1,9},{25,17},{17,25},{10,2},{2,... | collective-permute-start | bytes 614408 | tf_op jit(solution)/shard_map/ppermute | solution.py:333
  394.6 0.8 copy-start.8
  394.6 0.9 copy-start.9
  399.3 0.7 copy-start.10
  399.3 0.8 copy-start.11
  399.3 0.8 copy-start.12
